TPU v7x, 512 devices: a whole 4x4x16 slice. The times are simulated.
512 devices in a mesh: seq: 64 (over y, z), head: 8 (over x, core).
Axes of the slice: x: 4, y: 4, z: 16, core: 2. Of those that a mesh axis runs over, the one named last changes fastest.
Arguments:
- queries: bfloat16 [128, 4096], P(None, 'head'), may hold values from -400 to 400
- keys: bfloat16 [16384, 1024], P('seq', 'head'), may hold values from -6 to 6
- values: bfloat16 [16384, 1024], P('seq', 'head'), may hold values from -6 to 6
- householder: bfloat16 [16384, 1024], P('seq', 'head'), may hold values from -6 to 6
- out_proj: bfloat16 [4096, 4096], P('head', 'seq'), may hold values from -0.09375 to 0.09375
Outputs:
- mixed: bfloat16 [128, 4096], P('head', 'seq')
All inputs are finite; a program needn't handle non-finite values.
Results may differ from a plain program's by a relative error of at most 0.02.
Values may be sent and summed in bfloat16 or wider, within the bound.
A program may use at most 64 MiB of HBM per device.

v0:
```python
import jax
import jax.numpy as jnp
from jax import lax
from jax.sharding import PartitionSpec as P

BLOCK = 64


def merged(array, axis, combine):
    everything = jax.tree.map(lambda part: lax.all_gather(part, axis), array)
    initial = jax.tree.map(lambda part: part[0], everything)

    def turn(k, so_far):
        return combine(so_far, jax.tree.map(lambda part: part[k], everything))

    return lax.fori_loop(1, lax.axis_size(axis), turn, initial)


def unit_rows(raw_vecs):
    return raw_vecs * lax.rsqrt(jnp.sum(raw_vecs * raw_vecs, axis=-1, keepdims=True) + 1e-06)


def span_forms(raw_vecs, keys_float):
    precise = lax.Precision.HIGHEST
    vectors = unit_rows(raw_vecs)
    block_len = vectors.shape[1]
    head_width = vectors.shape[2]
    row_ids = lax.broadcasted_iota(jnp.int32, (block_len, block_len), 0)
    col_ids = lax.broadcasted_iota(jnp.int32, (block_len, block_len), 1)
    gram = jnp.einsum("nad,nbd->nab", vectors, vectors, precision=precise)
    lower = jnp.where(row_ids > col_ids, gram, 0.0) + jnp.where(row_ids == col_ids, 0.5, 0.0)
    identity_block = jnp.broadcast_to(jnp.eye(block_len, dtype=jnp.float32), lower.shape)
    coeff = jax.scipy.linalg.solve_triangular(lower, identity_block, lower=True)
    identity_head = jnp.eye(head_width, dtype=jnp.float32)
    transition = identity_head - jnp.einsum(
        "nad,nab,nbe->nde", vectors, coeff, vectors, precision=precise
    )
    inner = jnp.einsum("nbd,njd->nbj", vectors, keys_float, precision=precise)
    inner = jnp.where(row_ids > col_ids, inner, 0.0)
    mixing = jnp.einsum("nab,nbj->naj", coeff, inner, precision=precise)
    carried = keys_float - jnp.einsum("naj,nad->njd", mixing, vectors, precision=precise)
    return (transition, carried)


def carry_back(transition, carried, identity_head):
    precise = lax.Precision.HIGHEST

    def advance(running, span_item):
        factor, block_keys = span_item
        emitted = jnp.dot(block_keys, running.T, precision=precise)
        return (jnp.dot(running, factor, precision=precise), emitted)

    return lax.scan(advance, identity_head, (transition, carried), reverse=True)


def compose_batch(earlier, later):
    return jnp.einsum("nab,nbc->nac", earlier, later, precision=lax.Precision.HIGHEST)


def combine_parts(first, second):
    peak_one, total_one, numer_one = first
    peak_two, total_two, numer_two = second
    peak = jnp.maximum(peak_one, peak_two)
    factor_one = jnp.exp(peak_one - peak)
    factor_two = jnp.exp(peak_two - peak)
    return (
        peak,
        total_one * factor_one + total_two * factor_two,
        numer_one * factor_one[..., None] + numer_two * factor_two[..., None],
    )


def on_device(queries, keys, values, householder, out_proj):
    precise = lax.Precision.HIGHEST
    ctx_rows, head_width = keys.shape
    blocks = ctx_rows // BLOCK
    raw_vecs = householder.astype(jnp.float32).reshape(blocks, BLOCK, head_width)
    keys_float = keys.astype(jnp.float32).reshape(blocks, BLOCK, head_width)
    transition, carried = span_forms(raw_vecs, keys_float)
    identity_head = jnp.eye(head_width, dtype=jnp.float32)
    shard_mat, local_keys = carry_back(transition, carried, identity_head)
    local_keys = local_keys.reshape(ctx_rows, head_width)
    all_trans = lax.all_gather(shard_mat[None], "seq", axis=0, tiled=True)
    my_index = lax.axis_index("seq")
    inclusive = lax.associative_scan(compose_batch, all_trans, reverse=True)
    padded_stack = jnp.concatenate([inclusive, identity_head[None]], axis=0)
    suffix_mat = lax.dynamic_index_in_dim(padded_stack, my_index + 1, 0, keepdims=False)
    query_count = queries.shape[0]
    group_size = queries.shape[1] // head_width
    query_float = queries.astype(jnp.float32).reshape(query_count, group_size, head_width)
    turned = jnp.einsum("ihe,ef->hif", query_float, suffix_mat, precision=precise)
    inv_root = 1.0 / jnp.sqrt(jnp.float32(head_width))

    def attend(query_rows):
        scores = jnp.einsum("if,jf->ij", query_rows, local_keys, precision=precise) * inv_root
        peak = jnp.max(scores, axis=1)
        expo = jnp.exp(scores - peak[:, None])
        totals = jnp.sum(expo, axis=1)
        numerators = jnp.dot(expo.astype(jnp.bfloat16), values, preferred_element_type=jnp.float32)
        return (peak, totals, numerators)

    peaks, totals, numerators = lax.map(attend, turned)
    best, merged_total, merged_numer = merged((peaks, totals, numerators), "seq", combine_parts)
    attention = (merged_numer / merged_total[..., None]).astype(jnp.bfloat16)
    flat_attention = jnp.transpose(attention, (1, 0, 2)).reshape(
        query_count, group_size * head_width
    )
    return lax.psum_scatter(
        jnp.dot(flat_attention, out_proj, preferred_element_type=jnp.float32).astype(jnp.bfloat16),
        "head",
        scatter_dimension=0,
        tiled=True,
    )


def solution(mesh):
    placed = (
        P(None, "head"),
        P("seq", "head"),
        P("seq", "head"),
        P("seq", "head"),
        P("head", "seq"),
    )
    return jax.shard_map(
        on_device, mesh=mesh, in_specs=placed, out_specs=P("head", "seq"), check_vma=False
    )
```

profile of v0, /device:TPU:4, one launch (start us, length us, event | category | flops | bytes accessed | tf_op | source)
XLA Modules:
  0.0 591.6 jit_solution(18420621423005850482)
XLA Ops:
  7.8 1.3 fusion.24
  9.1 19.7 %custom-call.4 = f32[4,1,64,64]{2,3,1,0:T(8,128)S(1)} custom-call(f32[4,1,64,64]{3,2,1,0:T(8,128)S(1)} %fusion.24), custom_call_target="InvertDiagBlocksLowerTriangular" | custom-call | tf_op jit(solution)/shard_map/jit(_solve_triangular)/vmap()/triangular_solve | solution.py:33
  30.3 1.3 fusion.50
  33.9 2.1 while.49
  36.9 151.1 %all-gather.9.cloned.1.call-done = f32[8192,128]{1,0:T(8,128)} async-done(((f32[128,128]{1,0:T(8,128)}), f32[8192,128]{1,0:T(8,128)}) %all-gather.9.cloned.1.call-update) | async-done | bytes 4194320 | tf_op jit(solution)/shard_map/all_gather | solution.py:83
  188.0 3.1 slice.111
  191.1 1.7 slice.112
  192.9 3.7 fusion.18
  202.1 5.8 pad.43
  207.8 1.3 add.157
  211.4 10.2 %pad.46 = f32[32,128,128]{2,1,0:T(8,128)} pad(f32[16,128,128]{2,1,0:T(8,128)} %copy-done.3, f32[]{:T(128)} %constant.115.clone.1), padding=1_0_1x0_0_0x0_0_0 | pad | bytes 3145732 | tf_op jit(solution)/shard_map/pad | solution.py:85
  221.6 6.5 %pad.45 = f32[32,128,128]{2,1,0:T(8,128)} pad(f32[16,128,128]{2,1,0:T(8,128)S(1)} %pad_maximum_fusion.1, f32[]{:T(128)} %constant.115.clone.1), padding=0_1_1x0_0_0x0_0_0 | pad | bytes 3145732 | tf_op jit(solution)/shard_map/pad | solution.py:85
  228.1 2.5 add.158
  230.6 5.0 fusion.20
  235.5 12.1 %pad.48 = f32[64,128,128]{2,1,0:T(8,128)} pad(f32[32,128,128]{2,1,0:T(8,128)S(1)} %add.158, f32[]{:T(128)} %constant.115.clone.1), padding=1_0_1x0_0_0x0_0_0 | pad | bytes 6291460 | tf_op jit(solution)/shard_map/pad | solution.py:85
  248.5 1.7 pad_maximum_fusion
  250.2 12.1 %pad.47 = f32[64,128,128]{2,1,0:T(8,128)} pad(f32[32,128,128]{2,1,0:T(8,128)S(1)} %pad_maximum_fusion, f32[]{:T(128)} %constant.115.clone.1), padding=0_1_1x0_0_0x0_0_0 | pad | bytes 6291460 | tf_op jit(solution)/shard_map/pad | solution.py:85
  262.3 6.5 %add.159 = f32[64,128,128]{2,1,0:T(8,128)} add(f32[64,128,128]{2,1,0:T(8,128)} %pad.47, f32[64,128,128]{2,1,0:T(8,128)} %pad.48) | non-fusion elementwise | flops 1048576 | bytes 12582912 | tf_op jit(solution)/shard_map/add | solution.py:85
  268.8 4.6 rev.4
  274.6 6.0 %while.50 = (s32[]{:T(128)}, f32[4,128]{1,0:T(4,128)S(1)}, f32[4,128]{1,0:T(4,128)S(1)}, f32[4,128,128]{2,1,0:T(8,128)}, f32[4,128,128]{1,2,0:T(8,128)S(1)}, /*i...) while((s32[]{:T(128)}, f32[4,128]{1,0:T(4,128)S(1)}, ...), condition=%wide.region_6.7_spmd, body=%wide.region_3.6_spmd.sunk | while | flops 58916608 | bytes 725109 | solution.py:102
  280.7 97.9 %all-gather.4 = f32[64,4,128]{2,1,0:T(4,128)S(1)} all-gather(f32[1,4,128]{2,1,0:T(4,128)S(1)} %bitcast.152), channel_id=3, replica_groups=mesh['seq'=64,'head'=8] {'seq'}, dimensions={0}, use_global_device_ids=true | all-gather | bytes 133120 | tf_op jit(solution)/shard_map/all_gather | solution.py:10
  378.6 97.5 %all-gather.5 = f32[64,4,128]{2,1,0:T(4,128)S(1)} all-gather(f32[1,4,128]{2,1,0:T(4,128)S(1)} %bitcast.151), channel_id=4, replica_groups=mesh['seq'=64,'head'=8] {'seq'}, dimensions={0}, use_global_device_ids=true | all-gather | bytes 133120 | tf_op jit(solution)/shard_map/all_gather | solution.py:10
  477.1 79.3 %while.51 = (s32[]{:T(128)}, f32[4,128]{1,0:T(4,128)S(1)}, f32[4,128]{1,0:T(4,128)S(1)}, f32[4,128,128]{2,1,0:T(8,128)S(1)}, f32[64,4,128]{2,1,0:T(4,128)S(1)}, ...) while((s32[]{:T(128)}, f32[4,128]{1,0:T(4,128)S(1)}, ...), condition=%wide.region_8.9_spmd, body=%wide.region_7.8_spmd.sunk | while | flops 199685 | bytes 807055 | solution.py:16
  557.4 27.6 %reduce-scatter.2.cloned.1.call-done = bf16[16,64]{1,0:T(8,128)(2,1)} async-done(((bf16[128,64]{1,0:T(8,128)(2,1)}), bf16[16,64]{1,0:T(8,128)(2,1)}) %reduce-scatter.2.cloned.1.call-update) | async-done | bytes 2064 | tf_op jit(solution)/shard_map/reduce_scatter | solution.py:108
  (233 shorter events, 103.1 us)
Async XLA Ops:
  6.5 266.9 %copy-start = (bf16[128,512]{1,0:T(8,128)(2,1)S(1)}, bf16[128,512]{1,0:T(8,128)(2,1)}, u32[]{:S(2)}) copy-start(bf16[128,512]{1,0:T(8,128)(2,1)} %param.11) | copy-start | bytes 393220
  6.5 26.7 %copy-start.4 = (bf16[256,128]{1,0:T(8,128)(2,1)S(1)}, bf16[256,128]{1,0:T(8,128)(2,1)}, u32[]{:S(2)}) copy-start(bf16[256,128]{1,0:T(8,128)(2,1)} %param.14) | copy-start | bytes 196612
  6.5 181.4 %all-gather.9.cloned.1.call-start = ((), (), s32[]{:S(2)}) async-start(), calls=%async_computation.2 | async-start | bytes 4259840 | tf_op jit(solution)/shard_map/all_gather | solution.py:83
  36.8 439.3 %all-gather.11.cloned.1.call-start = ((), (), s32[]{:S(2)}) async-start(), calls=%async_computation.3 | async-start | bytes 17039360 | tf_op jit(solution)/shard_map/all_gather | solution.py:10
  196.6 1.9 copy-start.1
  202.1 8.2 %copy-start.2 = (f32[32,128,128]{2,1,0:T(8,128)S(1)}, f32[32,128,128]{2,1,0:T(8,128)}, u32[]{:S(2)}) copy-start(f32[32,128,128]{2,1,0:T(8,128)} %copy-done.1) | copy-start | bytes 6291460
  209.2 1.1 copy-start.3
  211.4 10.2 %slice-start = ((f32[32,128,128]{2,1,0:T(8,128)}), f32[1,128,128]{2,1,0:T(8,128)S(1)}, s32[]{:S(2)}) async-start(f32[32,128,128]{2,1,0:T(8,128)} %copy-done.1), calls=%async_computation.4 | async-start | bytes 131072 | tf_op jit(solution)/shard_map/slice | solution.py:85
  273.4 1.2 copy-start.5
  280.7 304.4 %reduce-scatter.2.cloned.1.call-start = ((), (), s32[]{:S(2)}) async-start(), calls=%async_computation.1 | async-start | bytes 36864 | tf_op jit(solution)/shard_map/reduce_scatter | solution.py:108
  477.1 79.5 %copy-start.6 = (bf16[512,64]{0,1:T(8,128)(2,1)S(1)}, bf16[512,64]{0,1:T(8,128)(2,1)}, u32[]{:S(2)}) copy-start(bf16[512,64]{0,1:T(8,128)(2,1)} %param.15) | copy-start | bytes 196612
Sparse Core Ops, SparseCore 0:
  36.9 151.0 all-gather.8
  280.8 188.8 all-gather.10
  557.6 27.4 reduce-scatter.1
where the time goes:
time: 600 us; the launch traced here: 592 us
  blocking collectives  195 us (32%)
  waiting for transfers between devices  179 us (30%)
  other arithmetic  112 us (19%)
  local copies, waits for them, and re-layouts  60.8 us (10%)
  matrix products  28.9 us (5%)
  between operations  13.6 us (2%)
    all_gather x2, blocking collectives, merged(): everything = jax.tree.map(lambda part: lax.all_gather(part, axis), array)  195 us
    all_gather x1, waiting for transfers between devices, on_device(): all_trans = lax.all_gather(shard_mat[None], 'seq', axis=0, tiled=True)  151 us
    add x63, other arithmetic, combine_parts(): numer_one * factor_one[..., None] + numer_two * factor_two[..., None]  76 us
    pad x10, local copies, waits for them, and re-layouts, on_device(): inclusive = lax.associative_scan(compose_batch, all_trans, reverse=True)  47.1 us
    reduce_scatter x1, waiting for transfers between devices, on_device(): lax.psum_scatter(jnp.dot(flat_attention, out_proj, preferred_element_type...  27.6 us
    another operation x1, other arithmetic, span_forms(): coeff = jax.scipy.linalg.solve_triangular(lower, identity_block, lower=True)  19.7 us
    dot_general x11, matrix products, compose_batch(): jnp.einsum('nab,nbc->nac', earlier, later, precision=lax.Precision.HIGHEST)  13.6 us
  transfers between devices with their start and end apart: 3, of which 2 were waited for; matrix products, arithmetic and copies ran while one was open for 0% of the time, Pallas kernels for 0%

commit v1 on v0

v1 whole, which is shorter than its diff:
```python
import jax
import jax.numpy as jnp
from jax import lax
from jax.experimental import pallas as pl
from jax.experimental.pallas import tpu as pltpu
from jax.sharding import PartitionSpec as P

F32 = jnp.float32
BF16 = jnp.bfloat16
MESH = pl.DeviceIdType.MESH
RADIX = 4
ROWS_Y = 4
ROWS_Z = 16
HEADS = 8
HEAD = 128
ML_ROWS = 16
SLAB = HEAD + ML_ROWS

NN = (((1,), (0,)), ((), ()))
NT = (((1,), (1,)), ((), ()))
TN = (((0,), (0,)), ((), ()))


def dot(a, b, dims=NN):
    return lax.dot_general(a, b, dims, preferred_element_type=F32)


def split(x):
    high = x.astype(BF16)
    return high, (x - high.astype(F32)).astype(BF16)


def dot3(a, b, dims=NN):
    return dot(a[0], b[0], dims) + (dot(a[0], b[1], dims) + dot(a[1], b[0], dims))


def parts3(x):
    first = x.astype(BF16).astype(F32)
    rest = x - first
    second = rest.astype(BF16).astype(F32)
    return first, second, rest - second


def local_kernel(keys_ref, house_ref, trans_ref, carried_ref):
    raw = house_ref[...].astype(F32)
    vectors = raw * lax.rsqrt(jnp.sum(raw * raw, axis=1, keepdims=True) + 1e-06)
    count = vectors.shape[0]
    vec = split(vectors)
    keys = keys_ref[...]
    rows = lax.broadcasted_iota(jnp.int32, (count, count), 0)
    cols = lax.broadcasted_iota(jnp.int32, (count, count), 1)
    gram = dot3(vec, vec, NT)
    strict = jnp.where(rows < cols, gram, 0.0)
    pair = (rows | 1) == (cols | 1)
    inverse = jnp.where(rows == cols, 2.0, 0.0) - jnp.where(pair, 4.0 * strict, 0.0)
    size = 2
    while 2 * size < count:
        below = (rows & -(2 * size)) == (cols & -(2 * size))
        below = below & ((rows & size) != (cols & size))
        coupling = split(jnp.where(below, strict, 0.0))
        inv = split(inverse)
        inverse = inverse - dot3(split(dot3(inv, coupling)), inv)
        size *= 2
    coupling = split(jnp.where((rows & size) != (cols & size), strict, 0.0))
    inv = split(inverse)
    half = dot3(inv, vec)
    weights = split(half - dot3(inv, split(dot3(coupling, split(half)))))
    eye_rows = lax.broadcasted_iota(jnp.int32, (HEAD, HEAD), 0)
    eye_cols = lax.broadcasted_iota(jnp.int32, (HEAD, HEAD), 1)
    identity = jnp.where(eye_rows == eye_cols, 1.0, 0.0)
    trans_high, trans_low = split(identity - dot3(weights, vec, TN))
    trans_ref[0] = trans_high
    trans_ref[1] = trans_low
    inner = dot(keys, vec[0], NT) + dot(keys, vec[1], NT)
    inner = split(jnp.where(rows < cols, inner, 0.0))
    carried_high, carried_low = split(keys.astype(F32) - dot3(inner, weights))
    carried_ref[0] = carried_high
    carried_ref[1] = carried_low


def chain(buf, last):
    products = [None] * RADIX
    running = (buf[RADIX - 1, 0], buf[RADIX - 1, 1])
    products[RADIX - 1] = running[0].astype(F32) + running[1].astype(F32)
    for i in range(RADIX - 2, last - 1, -1):
        products[i] = dot3(running, (buf[i, 0], buf[i, 1]))
        running = split(products[i])
    return products, running


def chosen(products, position):
    eye_rows = lax.broadcasted_iota(jnp.int32, (HEAD, HEAD), 0)
    eye_cols = lax.broadcasted_iota(jnp.int32, (HEAD, HEAD), 1)
    out = jnp.where(eye_rows == eye_cols, 1.0, 0.0)
    for i in range(RADIX - 1):
        out = jnp.where(position == i, products[i + 1], out)
    return out


def stat_rows(peak, total, rows):
    ids = lax.broadcasted_iota(jnp.int32, (rows, HEAD), 0)
    out = jnp.zeros((rows, HEAD), F32)
    for i, part in enumerate(parts3(peak) + parts3(total)):
        out = jnp.where(ids == i, part, out)
    return out


def remote_kernel(
    trans_ref, carried_ref, q_ref, v_ref, w_ref, o_ref,
    buf_a, buf_b, buf_y, slab_out, slab_in, part_out, part_in, att_z, att_y, mix_out, mix_in,
    sem_a, sem_b, sem_y, sem_sy, sem_sz, sem_gz, sem_gy, sem_h,
):
    seq = lax.axis_index("seq")
    head = lax.axis_index("head")
    y = lax.div(seq, ROWS_Z)
    z = lax.rem(seq, ROWS_Z)
    a = lax.div(z, RADIX)
    p = lax.rem(z, RADIX)
    started = []

    def y_peer(k):
        other = lax.rem(y + k, ROWS_Y)
        return other, (other * ROWS_Z + z, head)

    def z_peer(k):
        other = lax.rem(z + k, ROWS_Z)
        return other, (y * ROWS_Z + other, head)

    def a_peer(k):
        other = lax.rem(a + k, RADIX)
        return other, (y * ROWS_Z + other * RADIX + p, head)

    def p_peer(k):
        other = lax.rem(p + k, RADIX)
        return other, (y * ROWS_Z + a * RADIX + other, head)

    def head_peer(k):
        other = lax.rem(head + k, HEADS)
        return other, (seq, other)

    def exchange(peer, count, sems, source, target):
        copies = []
        for k in range(1, count):
            other, device = peer(k)
            copy = pltpu.make_async_remote_copy(
                src_ref=source(other), dst_ref=target,
                send_sem=sems.at[0, k], recv_sem=sems.at[1, k],
                device_id=device, device_id_type=MESH,
            )
            copy.start()
            copies.append(copy)
        started.extend(copies)
        return copies

    def arrived(copies):
        for copy in copies:
            copy.wait_recv()

    barrier = pltpu.get_barrier_semaphore()
    peers = 0
    for peer, count in ((z_peer, ROWS_Z), (y_peer, ROWS_Y), (head_peer, HEADS)):
        for k in range(1, count):
            pl.semaphore_signal(barrier, inc=1, device_id=peer(k)[1], device_id_type=MESH)
            peers += 1
    pl.semaphore_wait(barrier, peers)

    copies = exchange(p_peer, RADIX, sem_a, lambda other: trans_ref, buf_a.at[p])
    buf_a[p] = trans_ref[...]
    arrived(copies)
    products, full = chain(buf_a, 0)
    buf_b[a, 0] = full[0]
    buf_b[a, 1] = full[1]
    copies = exchange(a_peer, RADIX, sem_b, lambda other: buf_b.at[a], buf_b.at[a])
    after = split(chosen(products, p))
    arrived(copies)
    products, full = chain(buf_b, 0)
    buf_y[y, 0] = full[0]
    buf_y[y, 1] = full[1]
    copies = exchange(y_peer, ROWS_Y, sem_y, lambda other: buf_y.at[y], buf_y.at[y])
    after = split(dot3(split(chosen(products, a)), after))
    arrived(copies)
    products, _ = chain(buf_y, 1)
    suffix = split(dot3(split(chosen(products, y)), after))

    carried = (carried_ref[0], carried_ref[1])
    for h in range(RADIX):
        query = q_ref[:, h * HEAD:(h + 1) * HEAD]
        turned = split((dot(query, suffix[0]) + dot(query, suffix[1])) * (HEAD ** -0.5))
        scores = dot3(carried, turned, NT)
        peak = jnp.max(scores, axis=0, keepdims=True)
        expo = jnp.exp(scores - peak)
        total = jnp.sum(expo, axis=0, keepdims=True)
        numer = dot(v_ref[...], expo.astype(BF16), TN)
        slab_out[h, 0:HEAD, :] = numer.astype(BF16)
        slab_out[h, HEAD:SLAB, :] = stat_rows(peak, total, ML_ROWS).astype(BF16)

    copies = exchange(y_peer, ROWS_Y, sem_sy, lambda other: slab_out.at[other], slab_in.at[y])
    slab_in[y] = slab_out[y]
    arrived(copies)
    slabs = [slab_in[i].astype(F32) for i in range(ROWS_Y)]
    peaks = [s[HEAD:HEAD + 1] + s[HEAD + 1:HEAD + 2] + s[HEAD + 2:HEAD + 3] for s in slabs]
    totals = [s[HEAD + 3:HEAD + 4] + s[HEAD + 4:HEAD + 5] + s[HEAD + 5:HEAD + 6] for s in slabs]
    peak = jnp.maximum(jnp.maximum(peaks[0], peaks[1]), jnp.maximum(peaks[2], peaks[3]))
    factors = [jnp.exp(one - peak) for one in peaks]
    total = sum(f * t for f, t in zip(factors, totals))
    numer = sum(f * s[0:HEAD] for f, s in zip(factors, slabs))

    stats = jnp.broadcast_to(stat_rows(peak, total, 8)[None], (ROWS_Z, 8, HEAD))
    part_out[...] = jnp.concatenate([numer.reshape(ROWS_Z, 8, HEAD), stats], axis=1).astype(BF16)
    copies = exchange(z_peer, ROWS_Z, sem_sz, lambda other: part_out.at[other], part_in.at[z])
    part_in[z] = part_out[z]
    arrived(copies)
    parts = part_in[...].astype(F32)
    peaks = parts[:, 8:9] + parts[:, 9:10] + parts[:, 10:11]
    totals = parts[:, 11:12] + parts[:, 12:13] + parts[:, 13:14]
    factors = jnp.exp(peaks - jnp.max(peaks, axis=0, keepdims=True))
    total = jnp.sum(factors * totals, axis=0)
    numer = jnp.sum(factors * parts[:, 0:8], axis=0)
    mine = pl.ds(pl.multiple_of(z * 8, 8), 8)
    att_z[mine, :] = numer / total
    arrived(exchange(z_peer, ROWS_Z, sem_gz, lambda other: att_z.at[mine], att_z.at[mine]))
    att_y[y] = att_z[...].astype(BF16)
    arrived(exchange(y_peer, ROWS_Y, sem_gy, lambda other: att_y.at[y], att_y.at[y]))

    attention = att_y[...].reshape(RADIX * HEAD, HEAD)
    mixed = dot(attention, w_ref[...], TN)
    mix_out[...] = jnp.zeros(mix_out.shape, F32)
    mix_out[:, :, 0:mixed.shape[1]] = mixed.reshape(HEADS, HEAD // HEADS, mixed.shape[1])
    copies = exchange(head_peer, HEADS, sem_h, lambda other: mix_out.at[other], mix_in.at[head])
    mix_in[head] = mix_out[head]
    arrived(copies)
    o_ref[...] = jnp.sum(mix_in[...], axis=0)[:, 0:mixed.shape[1]].astype(BF16)
    for copy in started:
        copy.wait_send()


def on_device(queries, keys, values, householder, out_proj):
    count = keys.shape[0]
    vmem = pl.BlockSpec(memory_space=pltpu.VMEM)
    trans, carried = pl.pallas_call(
        local_kernel,
        out_shape=(
            jax.ShapeDtypeStruct((2, HEAD, HEAD), BF16),
            jax.ShapeDtypeStruct((2, count, HEAD), BF16),
        ),
        in_specs=[vmem] * 2,
        out_specs=(vmem, vmem),
        compiler_params=pltpu.CompilerParams(vmem_limit_bytes=32 * 1024 * 1024),
        name="local_transition",
    )(keys, householder)
    sems = [pltpu.SemaphoreType.DMA((2, n)) for n in (4, 4, 4, 4, 16, 16, 4, 8)]
    return pl.pallas_call(
        remote_kernel,
        out_shape=jax.ShapeDtypeStruct((HEAD // HEADS, out_proj.shape[1]), BF16),
        in_specs=[vmem] * 5,
        out_specs=vmem,
        scratch_shapes=[
            pltpu.VMEM((RADIX, 2, HEAD, HEAD), BF16),
            pltpu.VMEM((RADIX, 2, HEAD, HEAD), BF16),
            pltpu.VMEM((RADIX, 2, HEAD, HEAD), BF16),
            pltpu.VMEM((RADIX, SLAB, HEAD), BF16),
            pltpu.VMEM((ROWS_Y, SLAB, HEAD), BF16),
            pltpu.VMEM((ROWS_Z, 16, HEAD), BF16),
            pltpu.VMEM((ROWS_Z, 16, HEAD), BF16),
            pltpu.VMEM((HEAD, HEAD), F32),
            pltpu.VMEM((RADIX, HEAD, HEAD), BF16),
            pltpu.VMEM((HEADS, HEAD // HEADS, HEAD), F32),
            pltpu.VMEM((HEADS, HEAD // HEADS, HEAD), F32),
        ] + sems,
        compiler_params=pltpu.CompilerParams(
            collective_id=0, has_side_effects=True, vmem_limit_bytes=32 * 1024 * 1024
        ),
        name="suffix_attention",
    )(trans, carried, queries, values, out_proj)


def solution(mesh):
    placed = (
        P(None, "head"),
        P("seq", "head"),
        P("seq", "head"),
        P("seq", "head"),
        P("head", "seq"),
    )
    return jax.shard_map(
        on_device, mesh=mesh, in_specs=placed, out_specs=P("head", "seq"), check_vma=False
    )
```

time: 600 us -> 81.9 us (0.14)
  the two profiles are of different devices: /device:TPU:4 before, /device:TPU:1 now
where the time goes in v1:
time: 81.9 us; the launch traced here: 81.7 us
  Pallas kernels  80.1 us (98%)
  local copies, waits for them, and re-layouts  1.61 us (2%)
    pallas_call x1, Pallas kernels, on_device(): pl.pallas_call(remote_kernel, out_shape=jax.ShapeDtypeStruct((HEAD // HEA...  75.1 us
    pallas_call x1, Pallas kernels, on_device(): pl.pallas_call(local_kernel, out_shape=(jax.ShapeDtypeStruct((2, HEAD, HE...  5.02 us

profile of v1, /device:TPU:1, one launch (start us, length us, event | category | flops | bytes accessed | tf_op | source)
XLA Modules:
  0.0 81.7 jit_solution(7275624998169571524)
XLA Ops:
  0.0 0.0 copy-start.2
  0.0 0.0 copy-start.1
  0.0 0.0 copy-start
  0.0 1.0 %copy.6.w_ref = bf16[512,64]{1,0:T(8,128)(2,1)S(1)} copy(bf16[512,64]{0,1:T(8,128)(2,1)} %param.9) | data formatting | bytes 131072 | tf_op args[4]
  1.0 0.0 copy-done.2
  1.0 0.0 copy-done.1
  1.0 0.0 copy-start.3
  1.0 5.0 %local_transition.1 = (bf16[2,128,128]{2,1,0:T(8,128)(2,1)S(1)}, bf16[2,256,128]{2,1,0:T(8,128)(2,1)S(1)}) custom-call(bf16[256,128]{1,0:T(8,128)(2,1)S(1)} %copy-done.1, bf16[256,128]{1,0:T(8,128)(2,1)S(1)} %copy-done.2), custom_call_target="tpu_custom_call" | custom-call | tf_op jit(solution)/shard_map/local_transition/pallas_call | solution.py:240
  6.1 0.0 copy-done
  6.1 0.0 copy-done.3
  6.1 75.1 %suffix_attention.1 = bf16[16,64]{1,0:T(8,128)(2,1)S(1)} custom-call(bf16[2,128,128]{2,1,0:T(8,128)(2,1)S(1)} %get-tuple-element.7.trans_ref, bf16[2,256,128]{2,1,0:T(8,128)(2,1)S(1)} %get-tuple-element.8.carried_ref, bf16[128,512]{1,0:T(8,128)(2,1)S(1)} %copy-done, bf16[256,128]{1,0:T(8,128)(2,1)S(1)} %copy-done.3, bf16[512,64]{1,0:T(8,128)(2,1)S(1)} %copy.6.w_ref), custom_call_target="tpu_custom_call" | custom-call | tf_op jit(solution)/shard_map/suffix_attention/pallas_call | solution.py:252
  81.2 0.6 copy.8
Async XLA Ops:
  0.0 1.0 %copy-start.2 = (bf16[256,128]{1,0:T(8,128)(2,1)S(1)}, bf16[256,128]{1,0:T(8,128)(2,1)}, u32[]{:S(2)}) copy-start(bf16[256,128]{1,0:T(8,128)(2,1)} %house_ref.1) | copy-start | bytes 196612
  0.0 1.0 %copy-start.1 = (bf16[256,128]{1,0:T(8,128)(2,1)S(1)}, bf16[256,128]{1,0:T(8,128)(2,1)}, u32[]{:S(2)}) copy-start(bf16[256,128]{1,0:T(8,128)(2,1)} %keys_ref.1) | copy-start | bytes 196612
  0.0 6.1 %copy-start = (bf16[128,512]{1,0:T(8,128)(2,1)S(1)}, bf16[128,512]{1,0:T(8,128)(2,1)}, u32[]{:S(2)}) copy-start(bf16[128,512]{1,0:T(8,128)(2,1)} %q_ref.1) | copy-start | bytes 393220
  1.0 5.0 %copy-start.3 = (bf16[256,128]{1,0:T(8,128)(2,1)S(1)}, bf16[256,128]{1,0:T(8,128)(2,1)}, u32[]{:S(2)}) copy-start(bf16[256,128]{1,0:T(8,128)(2,1)} %v_ref.1) | copy-start | bytes 196612

commit v2 on v1

--- a/solution.py
+++ b/solution.py
@@ -41,12 +41,11 @@
     return first, second, rest - second
 
 
-def local_kernel(keys_ref, house_ref, trans_ref, carried_ref):
+def transition_of(house_ref):
     raw = house_ref[...].astype(F32)
     vectors = raw * lax.rsqrt(jnp.sum(raw * raw, axis=1, keepdims=True) + 1e-06)
     count = vectors.shape[0]
     vec = split(vectors)
-    keys = keys_ref[...]
     rows = lax.broadcasted_iota(jnp.int32, (count, count), 0)
     cols = lax.broadcasted_iota(jnp.int32, (count, count), 1)
     gram = dot3(vec, vec, NT)
@@ -65,17 +64,23 @@
     inv = split(inverse)
     half = dot3(inv, vec)
     weights = split(half - dot3(inv, split(dot3(coupling, split(half)))))
-    eye_rows = lax.broadcasted_iota(jnp.int32, (HEAD, HEAD), 0)
-    eye_cols = lax.broadcasted_iota(jnp.int32, (HEAD, HEAD), 1)
-    identity = jnp.where(eye_rows == eye_cols, 1.0, 0.0)
-    trans_high, trans_low = split(identity - dot3(weights, vec, TN))
-    trans_ref[0] = trans_high
-    trans_ref[1] = trans_low
+    return vec, weights, split(identity() - dot3(weights, vec, TN))
+
+
+def carried_keys(keys_ref, vec, weights):
+    keys = keys_ref[...]
+    count = keys.shape[0]
+    rows = lax.broadcasted_iota(jnp.int32, (count, count), 0)
+    cols = lax.broadcasted_iota(jnp.int32, (count, count), 1)
     inner = dot(keys, vec[0], NT) + dot(keys, vec[1], NT)
     inner = split(jnp.where(rows < cols, inner, 0.0))
-    carried_high, carried_low = split(keys.astype(F32) - dot3(inner, weights))
-    carried_ref[0] = carried_high
-    carried_ref[1] = carried_low
+    return split(keys.astype(F32) - dot3(inner, weights))
+
+
+def identity():
+    rows = lax.broadcasted_iota(jnp.int32, (HEAD, HEAD), 0)
+    cols = lax.broadcasted_iota(jnp.int32, (HEAD, HEAD), 1)
+    return jnp.where(rows == cols, 1.0, 0.0)
 
 
 def chain(buf, last):
@@ -89,9 +94,7 @@
 
 
 def chosen(products, position):
-    eye_rows = lax.broadcasted_iota(jnp.int32, (HEAD, HEAD), 0)
-    eye_cols = lax.broadcasted_iota(jnp.int32, (HEAD, HEAD), 1)
-    out = jnp.where(eye_rows == eye_cols, 1.0, 0.0)
+    out = identity()
     for i in range(RADIX - 1):
         out = jnp.where(position == i, products[i + 1], out)
     return out
@@ -105,10 +108,14 @@
     return out
 
 
-def remote_kernel(
-    trans_ref, carried_ref, q_ref, v_ref, w_ref, o_ref,
-    buf_a, buf_b, buf_y, slab_out, slab_in, part_out, part_in, att_z, att_y, mix_out, mix_in,
-    sem_a, sem_b, sem_y, sem_sy, sem_sz, sem_gz, sem_gy, sem_h,
+def far_first(count):
+    return sorted(range(1, count), key=lambda k: -min(k, count - k))
+
+
+def path_kernel(
+    q_ref, keys_ref, v_ref, house_ref, w_ref, o_ref,
+    buf_a, buf_b, buf_y, slab_out, slab_in, part_out, part_in, att_z, att_y, weight,
+    sem_a, sem_b, sem_c, sem_y, sem_w, sem_sy, sem_sz, sem_gz, sem_gy,
 ):
     seq = lax.axis_index("seq")
     head = lax.axis_index("head")
@@ -116,6 +123,8 @@
     z = lax.rem(seq, ROWS_Z)
     a = lax.div(z, RADIX)
     p = lax.rem(z, RADIX)
+    pair_head = lax.rem(lax.div(z, 2) - head + HEADS, HEADS)
+    stays = pair_head == head
     started = []
 
     def y_peer(k):
@@ -138,15 +147,22 @@
         other = lax.rem(head + k, HEADS)
         return other, (seq, other)
 
+    def merge_peer(k):
+        other = lax.rem(z + k, ROWS_Z)
+        owner = lax.rem(lax.div(other, 2) - head + HEADS, HEADS)
+        return 2 * owner + lax.rem(other, 2), (y * ROWS_Z + other, owner)
+
+    def send(source, target, send_sem, recv_sem, device):
+        return pltpu.make_async_remote_copy(
+            src_ref=source, dst_ref=target, send_sem=send_sem, recv_sem=recv_sem,
+            device_id=device, device_id_type=MESH,
+        )
+
     def exchange(peer, count, sems, source, target):
         copies = []
-        for k in range(1, count):
+        for k in far_first(count):
             other, device = peer(k)
-            copy = pltpu.make_async_remote_copy(
-                src_ref=source(other), dst_ref=target,
-                send_sem=sems.at[0, k], recv_sem=sems.at[1, k],
-                device_id=device, device_id_type=MESH,
-            )
+            copy = send(source(other), target, sems.at[0, k], sems.at[1, k], device)
             copy.start()
             copies.append(copy)
         started.extend(copies)
@@ -159,19 +175,43 @@
     barrier = pltpu.get_barrier_semaphore()
     peers = 0
     for peer, count in ((z_peer, ROWS_Z), (y_peer, ROWS_Y), (head_peer, HEADS)):
-        for k in range(1, count):
+        for k in far_first(count):
             pl.semaphore_signal(barrier, inc=1, device_id=peer(k)[1], device_id_type=MESH)
             peers += 1
-    pl.semaphore_wait(barrier, peers)
-
-    copies = exchange(p_peer, RADIX, sem_a, lambda other: trans_ref, buf_a.at[p])
-    buf_a[p] = trans_ref[...]
+    for k in far_first(ROWS_Z):
+        source = (y * ROWS_Z + lax.rem(z + k, ROWS_Z), pair_head)
+        pl.semaphore_signal(barrier, inc=1, device_id=source, device_id_type=MESH)
+        peers += 1
+
+    @pl.when(jnp.logical_not(stays))
+    def _():
+        pl.semaphore_signal(barrier, inc=1, device_id=(seq, pair_head), device_id_type=MESH)
+
+    vec, weights, trans = transition_of(house_ref)
+    buf_a[p, 0] = trans[0]
+    buf_a[p, 1] = trans[1]
+    pl.semaphore_wait(barrier, peers + 1 - stays.astype(jnp.int32))
+
+    copies = exchange(p_peer, RADIX, sem_a, lambda other: buf_a.at[p], buf_a.at[p])
+    weight_copies = exchange(head_peer, HEADS, sem_w, lambda other: w_ref, weight.at[head])
+    weight[head] = w_ref[...]
+    carried = carried_keys(keys_ref, vec, weights)
     arrived(copies)
     products, full = chain(buf_a, 0)
     buf_b[a, 0] = full[0]
     buf_b[a, 1] = full[1]
-    copies = exchange(a_peer, RADIX, sem_b, lambda other: buf_b.at[a], buf_b.at[a])
+    quarter = pl.ds(pl.multiple_of(p * 32, 32), 32)
+    slices = exchange(a_peer, RADIX, sem_b, lambda other: buf_b.at[a, :, quarter], buf_b.at[a, :, quarter])
     after = split(chosen(products, p))
+    copies = []
+    for k, piece in reversed(list(zip(far_first(RADIX), slices))):
+        piece.wait_recv()
+        source = buf_b.at[lax.rem(a + RADIX - k, RADIX), :, quarter]
+        for m in far_first(RADIX):
+            copy = send(source, source, sem_c.at[0, k, m], sem_c.at[1, k, m], p_peer(m)[1])
+            copy.start()
+            copies.append(copy)
+    started.extend(copies)
     arrived(copies)
     products, full = chain(buf_b, 0)
     buf_y[y, 0] = full[0]
@@ -182,7 +222,6 @@
     products, _ = chain(buf_y, 1)
     suffix = split(dot3(split(chosen(products, y)), after))
 
-    carried = (carried_ref[0], carried_ref[1])
     for h in range(RADIX):
         query = q_ref[:, h * HEAD:(h + 1) * HEAD]
         turned = split((dot(query, suffix[0]) + dot(query, suffix[1])) * (HEAD ** -0.5))
@@ -205,53 +244,57 @@
     total = sum(f * t for f, t in zip(factors, totals))
     numer = sum(f * s[0:HEAD] for f, s in zip(factors, slabs))
 
-    stats = jnp.broadcast_to(stat_rows(peak, total, 8)[None], (ROWS_Z, 8, HEAD))
-    part_out[...] = jnp.concatenate([numer.reshape(ROWS_Z, 8, HEAD), stats], axis=1).astype(BF16)
-    copies = exchange(z_peer, ROWS_Z, sem_sz, lambda other: part_out.at[other], part_in.at[z])
-    part_in[z] = part_out[z]
+    numer = numer.T.reshape(ROWS_Z, 8, HEAD)
+    stats = stat_rows(peak, total, HEAD).T.reshape(ROWS_Z, 8, HEAD)
+    part_out[...] = jnp.concatenate([numer, stats], axis=1).astype(BF16)
+    copies = exchange(merge_peer, ROWS_Z, sem_sz, lambda other: part_out.at[other], part_in.at[z])
+    own = 2 * pair_head + lax.rem(z, 2)
+    same_z = send(part_out.at[own], part_in.at[z], sem_sz.at[0, 0], sem_sz.at[1, 0], (seq, pair_head))
+
+    @pl.when(stays)
+    def _():
+        part_in[z] = part_out[own]
+
+    @pl.when(jnp.logical_not(stays))
+    def _():
+        same_z.start()
+        same_z.wait_recv()
+
     arrived(copies)
     parts = part_in[...].astype(F32)
-    peaks = parts[:, 8:9] + parts[:, 9:10] + parts[:, 10:11]
-    totals = parts[:, 11:12] + parts[:, 12:13] + parts[:, 13:14]
+    stats = parts[:, 8:16]
+    peaks = stats[:, :, 0:1] + stats[:, :, 1:2] + stats[:, :, 2:3]
+    totals = stats[:, :, 3:4] + stats[:, :, 4:5] + stats[:, :, 5:6]
     factors = jnp.exp(peaks - jnp.max(peaks, axis=0, keepdims=True))
     total = jnp.sum(factors * totals, axis=0)
     numer = jnp.sum(factors * parts[:, 0:8], axis=0)
-    mine = pl.ds(pl.multiple_of(z * 8, 8), 8)
+    mine = pl.ds(pl.multiple_of(pair_head * 16 + lax.rem(z, 2) * 8, 8), 8)
     att_z[mine, :] = numer / total
     arrived(exchange(z_peer, ROWS_Z, sem_gz, lambda other: att_z.at[mine], att_z.at[mine]))
     att_y[y] = att_z[...].astype(BF16)
     arrived(exchange(y_peer, ROWS_Y, sem_gy, lambda other: att_y.at[y], att_y.at[y]))
 
-    attention = att_y[...].reshape(RADIX * HEAD, HEAD)
-    mixed = dot(attention, w_ref[...], TN)
-    mix_out[...] = jnp.zeros(mix_out.shape, F32)
-    mix_out[:, :, 0:mixed.shape[1]] = mixed.reshape(HEADS, HEAD // HEADS, mixed.shape[1])
-    copies = exchange(head_peer, HEADS, sem_h, lambda other: mix_out.at[other], mix_in.at[head])
-    mix_in[head] = mix_out[head]
-    arrived(copies)
-    o_ref[...] = jnp.sum(mix_in[...], axis=0)[:, 0:mixed.shape[1]].astype(BF16)
+    arrived(weight_copies)
+    mixed = jnp.zeros(o_ref.shape, F32)
+    for g in range(HEADS):
+        rows = slice(g * 16, (g + 1) * 16)
+        attention = jnp.concatenate([att_y[i, rows, :] for i in range(ROWS_Y)], axis=1)
+        mixed = mixed + dot(attention, weight[g], NT)
+    o_ref[...] = mixed.astype(BF16)
     for copy in started:
         copy.wait_send()
 
+    @pl.when(jnp.logical_not(stays))
+    def _():
+        same_z.wait_send()
+
 
 def on_device(queries, keys, values, householder, out_proj):
-    count = keys.shape[0]
     vmem = pl.BlockSpec(memory_space=pltpu.VMEM)
-    trans, carried = pl.pallas_call(
-        local_kernel,
-        out_shape=(
-            jax.ShapeDtypeStruct((2, HEAD, HEAD), BF16),
-            jax.ShapeDtypeStruct((2, count, HEAD), BF16),
-        ),
-        in_specs=[vmem] * 2,
-        out_specs=(vmem, vmem),
-        compiler_params=pltpu.CompilerParams(vmem_limit_bytes=32 * 1024 * 1024),
-        name="local_transition",
-    )(keys, householder)
-    sems = [pltpu.SemaphoreType.DMA((2, n)) for n in (4, 4, 4, 4, 16, 16, 4, 8)]
+    rows, columns = out_proj.shape
     return pl.pallas_call(
-        remote_kernel,
-        out_shape=jax.ShapeDtypeStruct((HEAD // HEADS, out_proj.shape[1]), BF16),
+        path_kernel,
+        out_shape=jax.ShapeDtypeStruct((HEAD // HEADS, columns), BF16),
         in_specs=[vmem] * 5,
         out_specs=vmem,
         scratch_shapes=[
@@ -264,14 +307,13 @@
             pltpu.VMEM((ROWS_Z, 16, HEAD), BF16),
             pltpu.VMEM((HEAD, HEAD), F32),
             pltpu.VMEM((RADIX, HEAD, HEAD), BF16),
-            pltpu.VMEM((HEADS, HEAD // HEADS, HEAD), F32),
-            pltpu.VMEM((HEADS, HEAD // HEADS, HEAD), F32),
-        ] + sems,
+            pltpu.VMEM((HEADS, columns, rows), BF16),
+        ] + [pltpu.SemaphoreType.DMA(n) for n in ((2, 4), (2, 4), (2, 4, 4), (2, 4), (2, 8), (2, 4), (2, 16), (2, 16), (2, 4))],
         compiler_params=pltpu.CompilerParams(
             collective_id=0, has_side_effects=True, vmem_limit_bytes=32 * 1024 * 1024
         ),
-        name="suffix_attention",
-    )(trans, carried, queries, values, out_proj)
+        name="path_attention",
+    )(queries, keys, values, householder, out_proj.T)
 
 
 def solution(mesh):

time: 81.9 us -> 73.4 us (0.90)
  the two profiles are of different devices: /device:TPU:1 before, /device:TPU:4 now
where the time goes in v2:
time: 73.4 us; the launch traced here: 73.1 us
  Pallas kernels  68.3 us (93%)
  local copies, waits for them, and re-layouts  4.85 us (7%)
    pallas_call x1, Pallas kernels, on_device(): pl.pallas_call(path_kernel, out_shape=jax.ShapeDtypeStruct((HEAD // HEADS...  68.3 us
    unnamed x11, local copies, waits for them, and re-layouts  4.85 us

profile of v2, /device:TPU:4, one launch (start us, length us, event | category | flops | bytes accessed | tf_op | source)
XLA Modules:
  0.0 73.1 jit_solution(14028349647618242018)
XLA Ops:
  0.0 0.0 copy-start
  0.0 0.9 %copy-done = bf16[128,512]{1,0:T(8,128)(2,1)S(1)} copy-done((bf16[128,512]{1,0:T(8,128)(2,1)S(1)}, bf16[128,512]{1,0:T(8,128)(2,1)}, u32[]{:S(2)}) %copy-start) | copy-done | bytes 131096
  0.9 0.0 copy-start.1
  0.9 0.8 %copy-done.1 = bf16[256,128]{1,0:T(8,128)(2,1)S(1)} copy-done((bf16[256,128]{1,0:T(8,128)(2,1)S(1)}, bf16[256,128]{1,0:T(8,128)(2,1)}, u32[]{:S(2)}) %copy-start.1) | copy-done | bytes 65560
  1.7 0.0 copy-start.2
  1.7 0.8 %copy-done.2 = bf16[256,128]{1,0:T(8,128)(2,1)S(1)} copy-done((bf16[256,128]{1,0:T(8,128)(2,1)S(1)}, bf16[256,128]{1,0:T(8,128)(2,1)}, u32[]{:S(2)}) %copy-start.2) | copy-done | bytes 65560
  2.6 0.0 copy-start.3
  2.6 0.8 %copy-done.3 = bf16[256,128]{1,0:T(8,128)(2,1)S(1)} copy-done((bf16[256,128]{1,0:T(8,128)(2,1)S(1)}, bf16[256,128]{1,0:T(8,128)(2,1)}, u32[]{:S(2)}) %copy-start.3) | copy-done | bytes 65560
  3.4 0.0 copy-start.4
  3.4 0.8 %copy-done.4 = bf16[512,64]{0,1:T(8,128)(2,1)S(1)} copy-done((bf16[512,64]{0,1:T(8,128)(2,1)S(1)}, bf16[512,64]{0,1:T(8,128)(2,1)}, u32[]{:S(2)}) %copy-start.4) | copy-done | bytes 65560
  4.3 68.3 %path_attention.1 = bf16[16,64]{1,0:T(8,128)(2,1)S(1)} custom-call(bf16[128,512]{1,0:T(8,128)(2,1)S(1)} %copy-done, bf16[256,128]{1,0:T(8,128)(2,1)S(1)} %copy-done.1, bf16[256,128]{1,0:T(8,128)(2,1)S(1)} %copy-done.2, bf16[256,128]{1,0:T(8,128)(2,1)S(1)} %copy-done.3, bf16[64,512]{1,0:T(8,128)(2,1)S(1)} %bitcast.1), custom_call_target="tpu_custom_call" | custom-call | tf_op jit(solution)/shard_map/path_attention/pallas_call | solution.py:295
  72.5 0.6 copy.7
Async XLA Ops:
  0.0 0.9 %copy-start = (bf16[128,512]{1,0:T(8,128)(2,1)S(1)}, bf16[128,512]{1,0:T(8,128)(2,1)}, u32[]{:S(2)}) copy-start(bf16[128,512]{1,0:T(8,128)(2,1)} %q_ref.1) | copy-start | bytes 393220
  0.9 0.8 %copy-start.1 = (bf16[256,128]{1,0:T(8,128)(2,1)S(1)}, bf16[256,128]{1,0:T(8,128)(2,1)}, u32[]{:S(2)}) copy-start(bf16[256,128]{1,0:T(8,128)(2,1)} %keys_ref.1) | copy-start | bytes 196612
  1.7 0.8 %copy-start.2 = (bf16[256,128]{1,0:T(8,128)(2,1)S(1)}, bf16[256,128]{1,0:T(8,128)(2,1)}, u32[]{:S(2)}) copy-start(bf16[256,128]{1,0:T(8,128)(2,1)} %v_ref.1) | copy-start | bytes 196612
  2.6 0.8 %copy-start.3 = (bf16[256,128]{1,0:T(8,128)(2,1)S(1)}, bf16[256,128]{1,0:T(8,128)(2,1)}, u32[]{:S(2)}) copy-start(bf16[256,128]{1,0:T(8,128)(2,1)} %house_ref.1) | copy-start | bytes 196612
  3.4 0.8 %copy-start.4 = (bf16[512,64]{0,1:T(8,128)(2,1)S(1)}, bf16[512,64]{0,1:T(8,128)(2,1)}, u32[]{:S(2)}) copy-start(bf16[512,64]{0,1:T(8,128)(2,1)} %param.9) | copy-start | bytes 196612

commit v3 on v2

--- a/solution.py
+++ b/solution.py
@@ -31,7 +31,9 @@
 
 
 def dot3(a, b, dims=NN):
-    return dot(a[0], b[0], dims) + (dot(a[0], b[1], dims) + dot(a[1], b[0], dims))
+    left = jnp.concatenate([a[0], a[0], a[1]], axis=dims[0][0][0])
+    right = jnp.concatenate([b[0], b[1], b[0]], axis=dims[0][1][0])
+    return dot(left, right, dims)
 
 
 def parts3(x):
@@ -222,19 +224,25 @@
     products, _ = chain(buf_y, 1)
     suffix = split(dot3(split(chosen(products, y)), after))
 
-    for h in range(RADIX):
-        query = q_ref[:, h * HEAD:(h + 1) * HEAD]
+    copies = []
+    for k in far_first(ROWS_Y) + [0]:
+        h, device = y_peer(k)
+        query = q_ref[:, pl.ds(pl.multiple_of(h * HEAD, HEAD), HEAD)]
         turned = split((dot(query, suffix[0]) + dot(query, suffix[1])) * (HEAD ** -0.5))
         scores = dot3(carried, turned, NT)
         peak = jnp.max(scores, axis=0, keepdims=True)
         expo = jnp.exp(scores - peak)
         total = jnp.sum(expo, axis=0, keepdims=True)
-        numer = dot(v_ref[...], expo.astype(BF16), TN)
-        slab_out[h, 0:HEAD, :] = numer.astype(BF16)
-        slab_out[h, HEAD:SLAB, :] = stat_rows(peak, total, ML_ROWS).astype(BF16)
-
-    copies = exchange(y_peer, ROWS_Y, sem_sy, lambda other: slab_out.at[other], slab_in.at[y])
-    slab_in[y] = slab_out[y]
+        numer = dot(v_ref[...], expo.astype(BF16), TN).astype(BF16)
+        stats = stat_rows(peak, total, ML_ROWS).astype(BF16)
+        slab = slab_out.at[h] if k else slab_in.at[y]
+        slab[0:HEAD, :] = numer
+        slab[HEAD:SLAB, :] = stats
+        if k:
+            copy = send(slab, slab_in.at[y], sem_sy.at[0, k], sem_sy.at[1, k], device)
+            copy.start()
+            copies.append(copy)
+    started.extend(copies)
     arrived(copies)
     slabs = [slab_in[i].astype(F32) for i in range(ROWS_Y)]
     peaks = [s[HEAD:HEAD + 1] + s[HEAD + 1:HEAD + 2] + s[HEAD + 2:HEAD + 3] for s in slabs]

time: 73.4 us -> 72.6 us (0.989)
  Pallas kernels: 68.3 us -> 67.5 us
    pallas_call x1, Pallas kernels: 68.3 us -> 67.5 us  [on_device(): pl.pallas_call(path_kernel, out_shape=jax.ShapeDtypeStruct((HEAD // HEADS...]
where the time goes in v3:
time: 72.6 us; the launch traced here: 72.3 us
  Pallas kernels  67.5 us (93%)
  local copies, waits for them, and re-layouts  4.85 us (7%)
    pallas_call x1, Pallas kernels, on_device(): pl.pallas_call(path_kernel, out_shape=jax.ShapeDtypeStruct((HEAD // HEADS...  67.5 us
    unnamed x11, local copies, waits for them, and re-layouts  4.85 us

profile of v3, /device:TPU:4, one launch (start us, length us, event | category | flops | bytes accessed | tf_op | source)
XLA Modules:
  0.0 72.3 jit_solution(13029105883554509313)
XLA Ops:
  0.0 0.0 copy-start
  0.0 0.9 %copy-done = bf16[128,512]{1,0:T(8,128)(2,1)S(1)} copy-done((bf16[128,512]{1,0:T(8,128)(2,1)S(1)}, bf16[128,512]{1,0:T(8,128)(2,1)}, u32[]{:S(2)}) %copy-start) | copy-done | bytes 131096
  0.9 0.0 copy-start.1
  0.9 0.8 %copy-done.1 = bf16[256,128]{1,0:T(8,128)(2,1)S(1)} copy-done((bf16[256,128]{1,0:T(8,128)(2,1)S(1)}, bf16[256,128]{1,0:T(8,128)(2,1)}, u32[]{:S(2)}) %copy-start.1) | copy-done | bytes 65560
  1.7 0.0 copy-start.2
  1.7 0.8 %copy-done.2 = bf16[256,128]{1,0:T(8,128)(2,1)S(1)} copy-done((bf16[256,128]{1,0:T(8,128)(2,1)S(1)}, bf16[256,128]{1,0:T(8,128)(2,1)}, u32[]{:S(2)}) %copy-start.2) | copy-done | bytes 65560
  2.6 0.0 copy-start.3
  2.6 0.8 %copy-done.3 = bf16[256,128]{1,0:T(8,128)(2,1)S(1)} copy-done((bf16[256,128]{1,0:T(8,128)(2,1)S(1)}, bf16[256,128]{1,0:T(8,128)(2,1)}, u32[]{:S(2)}) %copy-start.3) | copy-done | bytes 65560
  3.4 0.0 copy-start.4
  3.4 0.8 %copy-done.4 = bf16[512,64]{0,1:T(8,128)(2,1)S(1)} copy-done((bf16[512,64]{0,1:T(8,128)(2,1)S(1)}, bf16[512,64]{0,1:T(8,128)(2,1)}, u32[]{:S(2)}) %copy-start.4) | copy-done | bytes 65560
  4.3 67.5 %path_attention.1 = bf16[16,64]{1,0:T(8,128)(2,1)S(1)} custom-call(bf16[128,512]{1,0:T(8,128)(2,1)S(1)} %copy-done, bf16[256,128]{1,0:T(8,128)(2,1)S(1)} %copy-done.1, bf16[256,128]{1,0:T(8,128)(2,1)S(1)} %copy-done.2, bf16[256,128]{1,0:T(8,128)(2,1)S(1)} %copy-done.3, bf16[64,512]{1,0:T(8,128)(2,1)S(1)} %bitcast.1), custom_call_target="tpu_custom_call" | custom-call | tf_op jit(solution)/shard_map/path_attention/pallas_call | solution.py:303
  71.7 0.6 copy.7
Async XLA Ops:
  0.0 0.9 %copy-start = (bf16[128,512]{1,0:T(8,128)(2,1)S(1)}, bf16[128,512]{1,0:T(8,128)(2,1)}, u32[]{:S(2)}) copy-start(bf16[128,512]{1,0:T(8,128)(2,1)} %q_ref.1) | copy-start | bytes 393220
  0.9 0.8 %copy-start.1 = (bf16[256,128]{1,0:T(8,128)(2,1)S(1)}, bf16[256,128]{1,0:T(8,128)(2,1)}, u32[]{:S(2)}) copy-start(bf16[256,128]{1,0:T(8,128)(2,1)} %keys_ref.1) | copy-start | bytes 196612
  1.7 0.8 %copy-start.2 = (bf16[256,128]{1,0:T(8,128)(2,1)S(1)}, bf16[256,128]{1,0:T(8,128)(2,1)}, u32[]{:S(2)}) copy-start(bf16[256,128]{1,0:T(8,128)(2,1)} %v_ref.1) | copy-start | bytes 196612
  2.6 0.8 %copy-start.3 = (bf16[256,128]{1,0:T(8,128)(2,1)S(1)}, bf16[256,128]{1,0:T(8,128)(2,1)}, u32[]{:S(2)}) copy-start(bf16[256,128]{1,0:T(8,128)(2,1)} %house_ref.1) | copy-start | bytes 196612
  3.4 0.8 %copy-start.4 = (bf16[512,64]{0,1:T(8,128)(2,1)S(1)}, bf16[512,64]{0,1:T(8,128)(2,1)}, u32[]{:S(2)}) copy-start(bf16[512,64]{0,1:T(8,128)(2,1)} %param.9) | copy-start | bytes 196612

commit v4 on v3

--- a/solution.py
+++ b/solution.py
@@ -176,27 +176,17 @@
 
     barrier = pltpu.get_barrier_semaphore()
     peers = 0
-    for peer, count in ((z_peer, ROWS_Z), (y_peer, ROWS_Y), (head_peer, HEADS)):
+    for peer, count in ((p_peer, RADIX), (a_peer, RADIX), (y_peer, ROWS_Y), (head_peer, HEADS)):
         for k in far_first(count):
             pl.semaphore_signal(barrier, inc=1, device_id=peer(k)[1], device_id_type=MESH)
             peers += 1
-    for k in far_first(ROWS_Z):
-        source = (y * ROWS_Z + lax.rem(z + k, ROWS_Z), pair_head)
-        pl.semaphore_signal(barrier, inc=1, device_id=source, device_id_type=MESH)
-        peers += 1
-
-    @pl.when(jnp.logical_not(stays))
-    def _():
-        pl.semaphore_signal(barrier, inc=1, device_id=(seq, pair_head), device_id_type=MESH)
 
     vec, weights, trans = transition_of(house_ref)
     buf_a[p, 0] = trans[0]
     buf_a[p, 1] = trans[1]
-    pl.semaphore_wait(barrier, peers + 1 - stays.astype(jnp.int32))
+    pl.semaphore_wait(barrier, peers)
 
     copies = exchange(p_peer, RADIX, sem_a, lambda other: buf_a.at[p], buf_a.at[p])
-    weight_copies = exchange(head_peer, HEADS, sem_w, lambda other: w_ref, weight.at[head])
-    weight[head] = w_ref[...]
     carried = carried_keys(keys_ref, vec, weights)
     arrived(copies)
     products, full = chain(buf_a, 0)
@@ -219,6 +209,8 @@
     buf_y[y, 0] = full[0]
     buf_y[y, 1] = full[1]
     copies = exchange(y_peer, ROWS_Y, sem_y, lambda other: buf_y.at[y], buf_y.at[y])
+    weight_copies = exchange(head_peer, HEADS, sem_w, lambda other: w_ref, weight.at[head])
+    weight[head] = w_ref[...]
     after = split(dot3(split(chosen(products, a)), after))
     arrived(copies)
     products, _ = chain(buf_y, 1)
@@ -255,6 +247,7 @@
     numer = numer.T.reshape(ROWS_Z, 8, HEAD)
     stats = stat_rows(peak, total, HEAD).T.reshape(ROWS_Z, 8, HEAD)
     part_out[...] = jnp.concatenate([numer, stats], axis=1).astype(BF16)
+    arrived(weight_copies)
     copies = exchange(merge_peer, ROWS_Z, sem_sz, lambda other: part_out.at[other], part_in.at[z])
     own = 2 * pair_head + lax.rem(z, 2)
     same_z = send(part_out.at[own], part_in.at[z], sem_sz.at[0, 0], sem_sz.at[1, 0], (seq, pair_head))
@@ -282,7 +275,6 @@
     att_y[y] = att_z[...].astype(BF16)
     arrived(exchange(y_peer, ROWS_Y, sem_gy, lambda other: att_y.at[y], att_y.at[y]))
 
-    arrived(weight_copies)
     mixed = jnp.zeros(o_ref.shape, F32)
     for g in range(HEADS):
         rows = slice(g * 16, (g + 1) * 16)

time: 72.6 us -> 71.4 us (0.983)
  the two profiles are of different devices: /device:TPU:4 before, /device:TPU:8 now
where the time goes in v4:
time: 71.4 us; the launch traced here: 71 us
  Pallas kernels  66.2 us (93%)
  local copies, waits for them, and re-layouts  4.85 us (7%)
    pallas_call x1, Pallas kernels, on_device(): pl.pallas_call(path_kernel, out_shape=jax.ShapeDtypeStruct((HEAD // HEADS...  66.2 us
    unnamed x11, local copies, waits for them, and re-layouts  4.85 us

profile of v4, /device:TPU:8, one launch (start us, length us, event | category | flops | bytes accessed | tf_op | source)
XLA Modules:
  0.0 71.0 jit_solution(8572542894227175633)
XLA Ops:
  0.0 0.0 copy-start
  0.0 0.9 %copy-done = bf16[128,512]{1,0:T(8,128)(2,1)S(1)} copy-done((bf16[128,512]{1,0:T(8,128)(2,1)S(1)}, bf16[128,512]{1,0:T(8,128)(2,1)}, u32[]{:S(2)}) %copy-start) | copy-done | bytes 131096
  0.9 0.0 copy-start.1
  0.9 0.8 %copy-done.1 = bf16[256,128]{1,0:T(8,128)(2,1)S(1)} copy-done((bf16[256,128]{1,0:T(8,128)(2,1)S(1)}, bf16[256,128]{1,0:T(8,128)(2,1)}, u32[]{:S(2)}) %copy-start.1) | copy-done | bytes 65560
  1.7 0.0 copy-start.2
  1.7 0.8 %copy-done.2 = bf16[256,128]{1,0:T(8,128)(2,1)S(1)} copy-done((bf16[256,128]{1,0:T(8,128)(2,1)S(1)}, bf16[256,128]{1,0:T(8,128)(2,1)}, u32[]{:S(2)}) %copy-start.2) | copy-done | bytes 65560
  2.6 0.0 copy-start.3
  2.6 0.8 %copy-done.3 = bf16[256,128]{1,0:T(8,128)(2,1)S(1)} copy-done((bf16[256,128]{1,0:T(8,128)(2,1)S(1)}, bf16[256,128]{1,0:T(8,128)(2,1)}, u32[]{:S(2)}) %copy-start.3) | copy-done | bytes 65560
  3.4 0.0 copy-start.4
  3.4 0.8 %copy-done.4 = bf16[512,64]{0,1:T(8,128)(2,1)S(1)} copy-done((bf16[512,64]{0,1:T(8,128)(2,1)S(1)}, bf16[512,64]{0,1:T(8,128)(2,1)}, u32[]{:S(2)}) %copy-start.4) | copy-done | bytes 65560
  4.3 66.2 %path_attention.1 = bf16[16,64]{1,0:T(8,128)(2,1)S(1)} custom-call(bf16[128,512]{1,0:T(8,128)(2,1)S(1)} %copy-done, bf16[256,128]{1,0:T(8,128)(2,1)S(1)} %copy-done.1, bf16[256,128]{1,0:T(8,128)(2,1)S(1)} %copy-done.2, bf16[256,128]{1,0:T(8,128)(2,1)S(1)} %copy-done.3, bf16[64,512]{1,0:T(8,128)(2,1)S(1)} %bitcast.1), custom_call_target="tpu_custom_call" | custom-call | tf_op jit(solution)/shard_map/path_attention/pallas_call | solution.py:295
  70.4 0.6 copy.7
Async XLA Ops:
  0.0 0.9 %copy-start = (bf16[128,512]{1,0:T(8,128)(2,1)S(1)}, bf16[128,512]{1,0:T(8,128)(2,1)}, u32[]{:S(2)}) copy-start(bf16[128,512]{1,0:T(8,128)(2,1)} %q_ref.1) | copy-start | bytes 393220
  0.9 0.8 %copy-start.1 = (bf16[256,128]{1,0:T(8,128)(2,1)S(1)}, bf16[256,128]{1,0:T(8,128)(2,1)}, u32[]{:S(2)}) copy-start(bf16[256,128]{1,0:T(8,128)(2,1)} %keys_ref.1) | copy-start | bytes 196612
  1.7 0.8 %copy-start.2 = (bf16[256,128]{1,0:T(8,128)(2,1)S(1)}, bf16[256,128]{1,0:T(8,128)(2,1)}, u32[]{:S(2)}) copy-start(bf16[256,128]{1,0:T(8,128)(2,1)} %v_ref.1) | copy-start | bytes 196612
  2.6 0.8 %copy-start.3 = (bf16[256,128]{1,0:T(8,128)(2,1)S(1)}, bf16[256,128]{1,0:T(8,128)(2,1)}, u32[]{:S(2)}) copy-start(bf16[256,128]{1,0:T(8,128)(2,1)} %house_ref.1) | copy-start | bytes 196612
  3.4 0.8 %copy-start.4 = (bf16[512,64]{0,1:T(8,128)(2,1)S(1)}, bf16[512,64]{0,1:T(8,128)(2,1)}, u32[]{:S(2)}) copy-start(bf16[512,64]{0,1:T(8,128)(2,1)} %param.9) | copy-start | bytes 196612

commit v5 on v4

--- a/solution.py
+++ b/solution.py
@@ -212,6 +212,7 @@
     weight_copies = exchange(head_peer, HEADS, sem_w, lambda other: w_ref, weight.at[head])
     weight[head] = w_ref[...]
     after = split(dot3(split(chosen(products, a)), after))
+    flipped = v_ref[...].astype(F32).T.astype(BF16)
     arrived(copies)
     products, _ = chain(buf_y, 1)
     suffix = split(dot3(split(chosen(products, y)), after))
@@ -225,7 +226,7 @@
         peak = jnp.max(scores, axis=0, keepdims=True)
         expo = jnp.exp(scores - peak)
         total = jnp.sum(expo, axis=0, keepdims=True)
-        numer = dot(v_ref[...], expo.astype(BF16), TN).astype(BF16)
+        numer = dot(flipped, expo.astype(BF16)).astype(BF16)
         stats = stat_rows(peak, total, ML_ROWS).astype(BF16)
         slab = slab_out.at[h] if k else slab_in.at[y]
         slab[0:HEAD, :] = numer
@@ -263,9 +264,12 @@
 
     arrived(copies)
     parts = part_in[...].astype(F32)
-    stats = parts[:, 8:16]
-    peaks = stats[:, :, 0:1] + stats[:, :, 1:2] + stats[:, :, 2:3]
-    totals = stats[:, :, 3:4] + stats[:, :, 4:5] + stats[:, :, 5:6]
+    stats = parts[:, 8:16].reshape(ROWS_Z * 8, HEAD).astype(BF16)
+    lanes = lax.broadcasted_iota(jnp.int32, (HEAD, 2 * HEAD), 0)
+    first = jnp.where(lax.broadcasted_iota(jnp.int32, (HEAD, 2 * HEAD), 1) < HEAD, 0, 3)
+    spread = dot(stats, jnp.where((lanes >= first) & (lanes < first + 3), 1.0, 0.0).astype(BF16))
+    peaks = spread[:, 0:HEAD].reshape(ROWS_Z, 8, HEAD)
+    totals = spread[:, HEAD:2 * HEAD].reshape(ROWS_Z, 8, HEAD)
     factors = jnp.exp(peaks - jnp.max(peaks, axis=0, keepdims=True))
     total = jnp.sum(factors * totals, axis=0)
     numer = jnp.sum(factors * parts[:, 0:8], axis=0)

time: 71.4 us -> 71.1 us (level)
  no operation moved by 1% of the time
where the time goes in v5:
time: 71.1 us; the launch traced here: 70.8 us
  Pallas kernels  66 us (93%)
  local copies, waits for them, and re-layouts  4.85 us (7%)
    pallas_call x1, Pallas kernels, on_device(): pl.pallas_call(path_kernel, out_shape=jax.ShapeDtypeStruct((HEAD // HEADS...  66 us
    unnamed x11, local copies, waits for them, and re-layouts  4.85 us

profile of v5, /device:TPU:8, one launch (start us, length us, event | category | flops | bytes accessed | tf_op | source)
XLA Modules:
  0.0 70.8 jit_solution(12705164460549872902)
XLA Ops:
  0.0 0.0 copy-start
  0.0 0.9 %copy-done = bf16[128,512]{1,0:T(8,128)(2,1)S(1)} copy-done((bf16[128,512]{1,0:T(8,128)(2,1)S(1)}, bf16[128,512]{1,0:T(8,128)(2,1)}, u32[]{:S(2)}) %copy-start) | copy-done | bytes 131096
  0.9 0.0 copy-start.1
  0.9 0.8 %copy-done.1 = bf16[256,128]{1,0:T(8,128)(2,1)S(1)} copy-done((bf16[256,128]{1,0:T(8,128)(2,1)S(1)}, bf16[256,128]{1,0:T(8,128)(2,1)}, u32[]{:S(2)}) %copy-start.1) | copy-done | bytes 65560
  1.7 0.0 copy-start.2
  1.7 0.8 %copy-done.2 = bf16[256,128]{1,0:T(8,128)(2,1)S(1)} copy-done((bf16[256,128]{1,0:T(8,128)(2,1)S(1)}, bf16[256,128]{1,0:T(8,128)(2,1)}, u32[]{:S(2)}) %copy-start.2) | copy-done | bytes 65560
  2.6 0.0 copy-start.3
  2.6 0.8 %copy-done.3 = bf16[256,128]{1,0:T(8,128)(2,1)S(1)} copy-done((bf16[256,128]{1,0:T(8,128)(2,1)S(1)}, bf16[256,128]{1,0:T(8,128)(2,1)}, u32[]{:S(2)}) %copy-start.3) | copy-done | bytes 65560
  3.4 0.0 copy-start.4
  3.4 0.8 %copy-done.4 = bf16[512,64]{0,1:T(8,128)(2,1)S(1)} copy-done((bf16[512,64]{0,1:T(8,128)(2,1)S(1)}, bf16[512,64]{0,1:T(8,128)(2,1)}, u32[]{:S(2)}) %copy-start.4) | copy-done | bytes 65560
  4.3 66.0 %path_attention.1 = bf16[16,64]{1,0:T(8,128)(2,1)S(1)} custom-call(bf16[128,512]{1,0:T(8,128)(2,1)S(1)} %copy-done, bf16[256,128]{1,0:T(8,128)(2,1)S(1)} %copy-done.1, bf16[256,128]{1,0:T(8,128)(2,1)S(1)} %copy-done.2, bf16[256,128]{1,0:T(8,128)(2,1)S(1)} %copy-done.3, bf16[64,512]{1,0:T(8,128)(2,1)S(1)} %bitcast.1), custom_call_target="tpu_custom_call" | custom-call | tf_op jit(solution)/shard_map/path_attention/pallas_call | solution.py:299
  70.2 0.6 copy.7
Async XLA Ops:
  0.0 0.9 %copy-start = (bf16[128,512]{1,0:T(8,128)(2,1)S(1)}, bf16[128,512]{1,0:T(8,128)(2,1)}, u32[]{:S(2)}) copy-start(bf16[128,512]{1,0:T(8,128)(2,1)} %q_ref.1) | copy-start | bytes 393220
  0.9 0.8 %copy-start.1 = (bf16[256,128]{1,0:T(8,128)(2,1)S(1)}, bf16[256,128]{1,0:T(8,128)(2,1)}, u32[]{:S(2)}) copy-start(bf16[256,128]{1,0:T(8,128)(2,1)} %keys_ref.1) | copy-start | bytes 196612
  1.7 0.8 %copy-start.2 = (bf16[256,128]{1,0:T(8,128)(2,1)S(1)}, bf16[256,128]{1,0:T(8,128)(2,1)}, u32[]{:S(2)}) copy-start(bf16[256,128]{1,0:T(8,128)(2,1)} %v_ref.1) | copy-start | bytes 196612
  2.6 0.8 %copy-start.3 = (bf16[256,128]{1,0:T(8,128)(2,1)S(1)}, bf16[256,128]{1,0:T(8,128)(2,1)}, u32[]{:S(2)}) copy-start(bf16[256,128]{1,0:T(8,128)(2,1)} %house_ref.1) | copy-start | bytes 196612
  3.4 0.8 %copy-start.4 = (bf16[512,64]{0,1:T(8,128)(2,1)S(1)}, bf16[512,64]{0,1:T(8,128)(2,1)}, u32[]{:S(2)}) copy-start(bf16[512,64]{0,1:T(8,128)(2,1)} %param.9) | copy-start | bytes 196612
